TPU v7x, 32 devices: a whole 2x2x4 slice. The times are simulated.
32 devices in a mesh: dp: 16 (over z, y, x), mp: 2 (over core).
Axes of the slice: x: 2, y: 2, z: 4, core: 2. Of those that a mesh axis runs over, the one named last changes fastest.
Arguments:
- features: bfloat16 [8, 512, 512], P(None, 'dp'), may hold values from -6 to 6
- token_ids: int32 [8, 512], P(None, 'dp'), may hold values from 0 to 80
- mel_target: bfloat16 [8, 512, 80], P(None, 'dp'), may hold values from -6 to 6
- token_target: int32 [8, 512], P(None, 'dp'), may hold values from 0 to 80
- segments: int32 [16, 512], replicated, may hold values from 0 to 511, as said below
- row_device: int32 [16], replicated, may hold values from 0 to 15, as said below
- offset_bucket: int32 [1023], replicated, may hold values from 0 to 319
- speech_weight: bfloat16 [512, 768], replicated, may hold values from -0.25 to 0.25
- speech_bias: float32 [768], replicated, may hold values from -3 to 3
- token_table: bfloat16 [81, 768], replicated, may hold values from -6 to 6
- first_gain: float32 [768], replicated, may hold values from 0.1 to 1.9
- first_shift: float32 [768], replicated, may hold values from -3 to 3
- query_weight: bfloat16 [768, 768], P(None, 'mp'), may hold values from -0.21875 to 0.21875
- key_weight: bfloat16 [768, 768], P(None, 'mp'), may hold values from -0.21875 to 0.21875
- value_weight: bfloat16 [768, 768], P(None, 'mp'), may hold values from -0.21875 to 0.21875
- bias_table: float32 [320, 12], P(None, 'mp'), may hold values from -4 to 4
- out_weight: bfloat16 [768, 768], P('mp'), may hold values from -0.875 to 0.875
- second_gain: float32 [768], replicated, may hold values from 0.1 to 1.9
- second_shift: float32 [768], replicated, may hold values from -3 to 3
- up_weight: bfloat16 [768, 3072], P(None, 'mp'), may hold values from -0.21875 to 0.21875
- up_bias: float32 [3072], P('mp'), may hold values from -3 to 3
- down_weight: bfloat16 [3072, 768], P('mp'), may hold values from -0.109375 to 0.109375
- down_bias: float32 [768], replicated, may hold values from -3 to 3
- mel_weight: bfloat16 [768, 80], replicated, may hold values from -0.21875 to 0.21875
- mel_bias: float32 [80], replicated, may hold values from -3 to 3
- vocab_weight: bfloat16 [768, 81], replicated, may hold values from -0.4375 to 0.4375
- vocab_bias: float32 [81], replicated, may hold values from -4 to 4
Outputs:
- mean_loss: float32 [], replicated
- feature_grad: bfloat16 [8, 512, 512], P(None, 'dp')
- speech_weight_grad: float32 [512, 768], replicated
- speech_bias_grad: float32 [768], replicated
- token_table_grad: float32 [81, 768], replicated
- first_gain_grad: float32 [768], replicated
- first_shift_grad: float32 [768], replicated
- query_weight_grad: float32 [768, 768], P(None, 'mp')
- key_weight_grad: float32 [768, 768], P(None, 'mp')
- value_weight_grad: float32 [768, 768], P(None, 'mp')
- bias_table_grad: float32 [320, 12], P(None, 'mp')
- out_weight_grad: float32 [768, 768], P('mp')
- second_gain_grad: float32 [768], replicated
- second_shift_grad: float32 [768], replicated
- up_weight_grad: float32 [768, 3072], P(None, 'mp')
- up_bias_grad: float32 [3072], P('mp')
- down_weight_grad: float32 [3072, 768], P('mp')
- down_bias_grad: float32 [768], replicated
- mel_weight_grad: float32 [768, 80], replicated
- mel_bias_grad: float32 [80], replicated
- vocab_weight_grad: float32 [768, 81], replicated
- vocab_bias_grad: float32 [81], replicated
Inputs may be any that keep to these rules, and one draw needn't show every extreme that they name: `segments`: along each row the ids start at 0 and never fall; a position attends to the positions of its row with its id. In every draw one speech row and one text row, chosen from the seed, hold one id over all 512 positions, and one other speech row starts a new id at every position. row_device[r] is the backbone index of row r. Rows below 8 are speech rows and go to indices below 8; text rows go to the others. No index receives more than 2 rows; in every draw some receive exactly 2 and some none.
All inputs are finite; a program needn't handle non-finite values.
Results may differ from a plain program's by a relative error of at most 0.015.
The roundings to bfloat16 on the way count: a program that leaves them out, or rounds other values in their place, can miss the bound.
Values may be sent and summed in bfloat16 or wider, within the bound.
No kernel may reach another device: no remote copies, remote signals or barrier semaphores. Data moves between devices by JAX's collectives and lax.ppermute only.
A program may use at most 192 MiB of HBM per device.

v0:
```python
import jax
import jax.numpy as jnp
from jax import lax
from jax.sharding import PartitionSpec as P

EPSILON = 1e-05
NEGATIVE = -1e30
HIGHEST = lax.Precision.HIGHEST


def contract_rows(left_side, right_side):
    return lax.dot_general(
        left_side, right_side, (((0,), (0,)), ((), ())), preferred_element_type=jnp.float32
    )


def times_transposed(left_side, right_side):
    return lax.dot_general(
        left_side, right_side, (((1,), (1,)), ((), ())), preferred_element_type=jnp.float32
    )


def matmul(left_side, right_side):
    return jnp.dot(left_side, right_side, preferred_element_type=jnp.float32)


def layer_norm(row_data, norm_gain, norm_shift):
    center = row_data - jnp.mean(row_data, axis=-1, keepdims=True)
    inverse = lax.rsqrt(jnp.mean(center * center, axis=-1, keepdims=True) + EPSILON)
    normal = center * inverse
    return (normal * norm_gain + norm_shift, normal, inverse)


def norm_back(grad_out, normal, inverse, norm_gain):
    scaled = grad_out * norm_gain
    grad_rows = inverse * (
        scaled
        - jnp.mean(scaled, axis=-1, keepdims=True)
        - normal * jnp.mean(scaled * normal, axis=-1, keepdims=True)
    )
    return (grad_rows, jnp.sum(grad_out * normal, axis=0), jnp.sum(grad_out, axis=0))


def smooth_gelu(hidden):
    return jax.nn.gelu(hidden, approximate=True)


def toeplitz(offsets, length):
    head_count = offsets.shape[0]
    widened = jnp.broadcast_to(offsets[:, None, :], (head_count, length, 2 * length - 1)).reshape(
        head_count, -1
    )
    widened = jnp.pad(widened, ((0, 0), (0, length)))
    return widened.reshape(head_count, length, 2 * length)[:, :, :length][:, :, ::-1]


def diagonal_sums(score_grid, length):
    head_count = score_grid.shape[0]
    sheared = jnp.pad(score_grid[:, :, ::-1], ((0, 0), (0, 0), (0, length))).reshape(head_count, -1)
    return jnp.sum(
        sheared[:, : length * (2 * length - 1)].reshape(head_count, length, 2 * length - 1), axis=1
    )


def row_scores(queries, key_rows, row_segment, pair_bias, scaling):
    raw_scores = (
        jnp.einsum("qhd,khd->hqk", queries, key_rows, preferred_element_type=jnp.float32) * scaling
    )
    same_segment = row_segment[:, None] == row_segment[None, :]
    return jnp.where(same_segment[None], raw_scores + pair_bias, NEGATIVE)


def to_slots(row_data, row_of_slot, slot_used, devices, capacity):
    picked = jnp.take(row_data, row_of_slot, axis=0)
    used_mask = slot_used.reshape((-1,) + (1,) * (row_data.ndim - 1))
    picked = jnp.where(used_mask, picked, jnp.zeros((), row_data.dtype))
    return picked.reshape((devices, capacity) + row_data.shape[1:])


def for_return(slot_data, devices):
    return slot_data.reshape(
        (1, slot_data.shape[0], devices, slot_data.shape[1] // devices) + slot_data.shape[2:]
    )


def speech_embed(feature_rows, speech_weight, speech_bias):
    return matmul(feature_rows, speech_weight) + speech_bias


def token_hot(token_list, vocab_size):
    return (token_list[:, None] == jnp.arange(vocab_size)[None, :]).astype(jnp.bfloat16)


def mel_loss(final_low, target, mel_weight, mel_bias, weighting):
    predicted = matmul(final_low, mel_weight) + mel_bias
    mel_error = predicted - target.astype(jnp.float32)
    smooth = jnp.sqrt(mel_error * mel_error + 1.0)
    return (
        jnp.sum((smooth - 1.0) * weighting),
        (mel_error / smooth * weighting).astype(jnp.bfloat16),
    )


def vocab_loss(final_low, labels, vocab_weight, vocab_bias, weighting):
    logits = matmul(final_low, vocab_weight) + vocab_bias
    shifted = logits - jnp.max(logits, axis=-1, keepdims=True)
    powers = jnp.exp(shifted)
    totals = jnp.sum(powers, axis=-1, keepdims=True)
    label_hot = (labels[:, None] == jnp.arange(logits.shape[1])[None, :]).astype(jnp.float32)
    losses = jnp.log(totals) - jnp.sum(shifted * label_hot, axis=-1, keepdims=True)
    return (
        jnp.sum(losses * weighting),
        ((powers / totals - label_hot) * weighting).astype(jnp.bfloat16),
    )


def per_device(
    features,
    token_ids,
    mel_target,
    token_target,
    segments,
    row_device,
    offset_bucket,
    speech_weight,
    speech_bias,
    token_table,
    first_gain,
    first_shift,
    query_weight,
    key_weight,
    value_weight,
    bias_table,
    out_weight,
    second_gain,
    second_shift,
    up_weight,
    up_bias,
    down_weight,
    down_bias,
    mel_weight,
    mel_bias,
    vocab_weight,
    vocab_bias,
):
    devices = lax.axis_size("dp")
    device_index = lax.axis_index("dp")
    rows_speech, part_len, feat_width = features.shape
    rows_text = token_ids.shape[0]
    rows_total, length = segments.shape
    capacity = 2 * rows_total // devices
    model_width = speech_weight.shape[1]
    vocab_size = token_table.shape[0]
    mel_width = mel_weight.shape[1]
    local_heads = bias_table.shape[1]
    head_size = query_weight.shape[1] // local_heads
    scaling = head_size ** (-0.5)
    tokens = capacity * length
    shaped = (capacity, length, local_heads, head_size)
    flat_heads = (tokens, local_heads * head_size)
    row_order = jnp.arange(rows_total)
    earlier = (row_device[:, None] == row_device[None, :]) & (
        row_order[None, :] < row_order[:, None]
    )
    slot_of_row = row_device * capacity + jnp.sum(earlier.astype(jnp.int32), axis=1)
    matches = slot_of_row[None, :] == jnp.arange(devices * capacity)[:, None]
    row_of_slot = jnp.sum(jnp.where(matches, row_order[None, :], 0), axis=1)
    slot_used = jnp.any(matches, axis=1)
    my_rows = lax.dynamic_slice_in_dim(row_of_slot, device_index * capacity, capacity)
    my_segments = jnp.take(segments, my_rows, axis=0)
    bucket_hot = (offset_bucket[:, None] == jnp.arange(bias_table.shape[0])[None, :]).astype(
        jnp.float32
    )
    offset_bias = jnp.dot(bucket_hot, bias_table, precision=HIGHEST)
    pair_bias = toeplitz(offset_bias.T, length)
    speech_low = (
        speech_embed(features.reshape(-1, feat_width), speech_weight, speech_bias)
        .astype(jnp.bfloat16)
        .reshape(rows_speech, part_len, model_width)
    )
    hot_ids = token_hot(token_ids.reshape(-1), vocab_size)
    text_low = (
        matmul(hot_ids, token_table).astype(jnp.bfloat16).reshape(rows_text, part_len, model_width)
    )
    embedded = jnp.concatenate([speech_low, text_low], axis=0)
    arrived = lax.all_to_all(
        to_slots(embedded, row_of_slot, slot_used, devices, capacity),
        "dp",
        split_axis=0,
        concat_axis=2,
        tiled=True,
    )
    flat_rows = (
        arrived.reshape(capacity, length, model_width)
        .reshape(tokens, model_width)
        .astype(jnp.float32)
    )
    norm_one, normal_one, inverse_one = layer_norm(flat_rows, first_gain, first_shift)
    norm_one_low = norm_one.astype(jnp.bfloat16)
    queries = matmul(norm_one_low, query_weight).astype(jnp.bfloat16)
    key_rows = matmul(norm_one_low, key_weight).astype(jnp.bfloat16)
    value_rows = matmul(norm_one_low, value_weight).astype(jnp.bfloat16)

    def attend_row(packed):
        row_queries, row_keys, row_values, row_segment = packed
        scores = row_scores(row_queries, row_keys, row_segment, pair_bias, scaling)
        highest = jnp.max(scores, axis=-1, keepdims=True)
        powers = jnp.exp(scores - highest)
        totals = jnp.sum(powers, axis=-1, keepdims=True)
        weights_low = (powers / totals).astype(jnp.bfloat16)
        heads_out = jnp.einsum(
            "hqk,khd->qhd", weights_low, row_values, preferred_element_type=jnp.float32
        )
        return (heads_out.astype(jnp.bfloat16), highest + jnp.log(totals))

    heads_low, log_totals = lax.map(
        attend_row,
        (
            queries.reshape(shaped),
            key_rows.reshape(shaped),
            value_rows.reshape(shaped),
            my_segments,
        ),
    )
    heads_flat = heads_low.reshape(flat_heads)
    attended = lax.psum(matmul(heads_flat, out_weight), "mp")
    mixed_rows = flat_rows + attended
    norm_two, normal_two, inverse_two = layer_norm(mixed_rows, second_gain, second_shift)
    norm_two_low = norm_two.astype(jnp.bfloat16)
    hidden = matmul(norm_two_low, up_weight) + up_bias
    active_low = smooth_gelu(hidden).astype(jnp.bfloat16)
    branch = lax.psum(matmul(active_low, down_weight), "mp")
    final_sum = mixed_rows + branch + down_bias
    kept_state = (
        normal_one,
        inverse_one,
        norm_one_low,
        queries,
        key_rows,
        value_rows,
        log_totals,
        heads_flat,
        normal_two,
        inverse_two,
        norm_two_low,
        hidden,
        active_low,
    )
    final_low, kept_state = (
        final_sum.astype(jnp.bfloat16).reshape(capacity, length, model_width),
        kept_state,
    )
    came_back = lax.all_to_all(
        for_return(final_low, devices), "dp", split_axis=2, concat_axis=0, tiled=True
    )
    final_rows = jnp.take(
        came_back.reshape(devices * capacity, part_len, model_width), slot_of_row, axis=0
    )
    speech_final = final_rows[:rows_speech].reshape(-1, model_width)
    text_final = final_rows[rows_speech:].reshape(-1, model_width)
    mel_sum, grad_predicted = mel_loss(
        speech_final,
        mel_target.reshape(-1, mel_width),
        mel_weight,
        mel_bias,
        1.0 / (mel_width * length),
    )
    text_sum, grad_logits = vocab_loss(
        text_final, token_target.reshape(-1), vocab_weight, vocab_bias, 1.0 / length
    )
    grad_mel_weight = contract_rows(speech_final, grad_predicted)
    grad_mel_bias = jnp.sum(grad_predicted.astype(jnp.float32), axis=0)
    grad_vocab_weight = contract_rows(text_final, grad_logits)
    grad_vocab_bias = jnp.sum(grad_logits.astype(jnp.float32), axis=0)
    grad_rows = jnp.concatenate(
        [
            times_transposed(grad_predicted, mel_weight).astype(jnp.bfloat16),
            times_transposed(grad_logits, vocab_weight).astype(jnp.bfloat16),
        ],
        axis=0,
    ).reshape(rows_total, part_len, model_width)
    sent_grads = lax.all_to_all(
        to_slots(grad_rows, row_of_slot, slot_used, devices, capacity),
        "dp",
        split_axis=0,
        concat_axis=2,
        tiled=True,
    )
    (
        normal_one,
        inverse_one,
        norm_one_low,
        queries,
        key_rows,
        value_rows,
        log_totals,
        heads_flat,
        normal_two,
        inverse_two,
        norm_two_low,
        hidden,
        active_low,
    ) = kept_state
    grad_final = sent_grads.reshape(capacity, length, model_width).reshape(tokens, model_width)
    grad_down = contract_rows(active_low, grad_final)
    grad_down_bias = jnp.sum(grad_final.astype(jnp.float32), axis=0)
    grad_active = times_transposed(grad_final, down_weight)
    gelu_back = jax.vjp(smooth_gelu, hidden)[1]
    grad_hidden_low = gelu_back(grad_active)[0].astype(jnp.bfloat16)
    grad_up = contract_rows(norm_two_low, grad_hidden_low)
    grad_up_bias = jnp.sum(grad_hidden_low.astype(jnp.float32), axis=0)
    grad_norm_two = lax.psum(
        times_transposed(grad_hidden_low, up_weight).astype(jnp.bfloat16), "mp"
    ).astype(jnp.float32)
    grad_mixed_part, grad_second_gain, grad_second_shift = norm_back(
        grad_norm_two, normal_two, inverse_two, second_gain
    )
    grad_mixed = grad_final.astype(jnp.float32) + grad_mixed_part
    grad_mixed_low = grad_mixed.astype(jnp.bfloat16)
    grad_out = contract_rows(heads_flat, grad_mixed_low)
    grad_heads_low = times_transposed(grad_mixed_low, out_weight).astype(jnp.bfloat16)

    def attend_back(packed):
        row_queries, row_keys, row_values, row_segment, row_log, row_grad = packed
        scores = row_scores(row_queries, row_keys, row_segment, pair_bias, scaling)
        weights = jnp.exp(scores - row_log)
        grad_weights = jnp.einsum(
            "qhd,khd->hqk", row_grad, row_values, preferred_element_type=jnp.float32
        )
        grad_scores = weights * (
            grad_weights - jnp.sum(weights * grad_weights, axis=-1, keepdims=True)
        )
        grad_low = grad_scores.astype(jnp.bfloat16)
        grad_queries = (
            jnp.einsum("hqk,khd->qhd", grad_low, row_keys, preferred_element_type=jnp.float32)
            * scaling
        ).astype(jnp.bfloat16)
        grad_keys = (
            jnp.einsum("hqk,qhd->khd", grad_low, row_queries, preferred_element_type=jnp.float32)
            * scaling
        ).astype(jnp.bfloat16)
        grad_values = jnp.einsum(
            "hqk,qhd->khd",
            weights.astype(jnp.bfloat16),
            row_grad,
            preferred_element_type=jnp.float32,
        ).astype(jnp.bfloat16)
        return (grad_queries, grad_keys, grad_values, diagonal_sums(grad_scores, length))

    results = lax.map(
        attend_back,
        (
            queries.reshape(shaped),
            key_rows.reshape(shaped),
            value_rows.reshape(shaped),
            my_segments,
            log_totals,
            grad_heads_low.reshape(shaped),
        ),
    )
    grad_queries = results[0].reshape(flat_heads)
    grad_keys = results[1].reshape(flat_heads)
    grad_values = results[2].reshape(flat_heads)
    grad_offsets = jnp.sum(results[3], axis=0)
    grad_table = jnp.dot(bucket_hot.T, grad_offsets.T, precision=HIGHEST)
    grad_query = contract_rows(norm_one_low, grad_queries)
    grad_key = contract_rows(norm_one_low, grad_keys)
    grad_value = contract_rows(norm_one_low, grad_values)
    grad_norm_one = lax.psum(
        (
            times_transposed(grad_queries, query_weight)
            + times_transposed(grad_keys, key_weight)
            + times_transposed(grad_values, value_weight)
        ).astype(jnp.bfloat16),
        "mp",
    ).astype(jnp.float32)
    grad_in_part, grad_first_gain, grad_first_shift = norm_back(
        grad_norm_one, normal_one, inverse_one, first_gain
    )
    grad_embedded_low = (
        (grad_mixed + grad_in_part).astype(jnp.bfloat16).reshape(capacity, length, model_width)
    )
    grad_embedded_low, block_grads = (
        grad_embedded_low,
        (
            grad_down,
            grad_down_bias,
            grad_up,
            grad_up_bias,
            grad_second_gain,
            grad_second_shift,
            grad_out,
            grad_query,
            grad_key,
            grad_value,
            grad_table,
            grad_first_gain,
            grad_first_shift,
        ),
    )
    grad_back = lax.all_to_all(
        for_return(grad_embedded_low, devices), "dp", split_axis=2, concat_axis=0, tiled=True
    )
    grad_rows_in = jnp.take(
        grad_back.reshape(devices * capacity, part_len, model_width), slot_of_row, axis=0
    )
    speech_grad = grad_rows_in[:rows_speech].reshape(-1, model_width)
    text_grad = grad_rows_in[rows_speech:].reshape(-1, model_width)
    grad_speech_weight = contract_rows(features.reshape(-1, feat_width), speech_grad)
    grad_speech_bias = jnp.sum(speech_grad.astype(jnp.float32), axis=0)
    grad_token_table = contract_rows(hot_ids, text_grad)
    feature_grad = (
        times_transposed(speech_grad, speech_weight)
        .astype(jnp.bfloat16)
        .reshape(rows_speech, part_len, feat_width)
    )
    local_loss = mel_sum + text_sum
    (
        grad_down,
        grad_down_bias,
        grad_up,
        grad_up_bias,
        grad_second_gain,
        grad_second_shift,
        grad_out,
        grad_query,
        grad_key,
        grad_value,
        grad_table,
        grad_first_gain,
        grad_first_shift,
    ) = block_grads
    (
        grad_down,
        grad_down_bias,
        grad_up,
        grad_up_bias,
        grad_second_gain,
        grad_second_shift,
        grad_mel_weight,
        grad_mel_bias,
        grad_vocab_weight,
        grad_vocab_bias,
        loss_total,
        grad_out,
        grad_query,
        grad_key,
        grad_value,
        grad_table,
        grad_first_gain,
        grad_first_shift,
        grad_speech_weight,
        grad_speech_bias,
        grad_token_table,
    ) = lax.psum(
        (
            grad_down,
            grad_down_bias,
            grad_up,
            grad_up_bias,
            grad_second_gain,
            grad_second_shift,
            grad_mel_weight,
            grad_mel_bias,
            grad_vocab_weight,
            grad_vocab_bias,
            local_loss,
            grad_out,
            grad_query,
            grad_key,
            grad_value,
            grad_table,
            grad_first_gain,
            grad_first_shift,
            grad_speech_weight,
            grad_speech_bias,
            grad_token_table,
        ),
        "dp",
    )
    return (
        loss_total / rows_total,
        feature_grad,
        grad_speech_weight,
        grad_speech_bias,
        grad_token_table,
        grad_first_gain,
        grad_first_shift,
        grad_query,
        grad_key,
        grad_value,
        grad_table,
        grad_out,
        grad_second_gain,
        grad_second_shift,
        grad_up,
        grad_up_bias,
        grad_down,
        grad_down_bias,
        grad_mel_weight,
        grad_mel_bias,
        grad_vocab_weight,
        grad_vocab_bias,
    )


def solution(mesh):
    placed = (
        P(None, "dp", None),
        P(None, "dp"),
        P(None, "dp", None),
        P(None, "dp"),
        P(),
        P(),
        P(),
        P(),
        P(),
        P(),
        P(),
        P(),
        P(None, "mp"),
        P(None, "mp"),
        P(None, "mp"),
        P(None, "mp"),
        P("mp", None),
        P(),
        P(),
        P(None, "mp"),
        P("mp"),
        P("mp", None),
        P(),
        P(),
        P(),
        P(),
        P(),
    )
    return jax.shard_map(
        per_device,
        mesh=mesh,
        in_specs=placed,
        out_specs=(
            P(),
            P(None, "dp", None),
            P(),
            P(),
            P(),
            P(),
            P(),
            P(None, "mp"),
            P(None, "mp"),
            P(None, "mp"),
            P(None, "mp"),
            P("mp", None),
            P(),
            P(),
            P(None, "mp"),
            P("mp"),
            P("mp", None),
            P(),
            P(),
            P(),
            P(),
            P(),
        ),
        check_vma=False,
    )
```

profile of v0, /device:TPU:0, one launch (start us, length us, event | category | flops | bytes accessed | tf_op | source)
XLA Modules:
  0.0 1292.0 jit_solution(15319664088204455640)
XLA Ops:
  33.3 13.6 %reshape.489 = f32[3142656]{0:T(1024)} reshape(f32[6,512,1023]{2,1,0:T(8,128)} %broadcast_in_dim.178) | data formatting | bytes 25141248
  47.0 14.0 %reshape.413 = f32[6,523776]{1,0:T(8,128)} reshape(f32[3142656]{0:T(1024)} %reshape.489) | data formatting | bytes 25141248 | tf_op jit(solution)/shard_map/reshape | solution.py:50
  61.0 11.8 pad.11
  72.8 17.6 %copy.197 = f32[1,6,512,1024]{3,2,1,0:T(8,128)} copy(f32[1,6,512,1024]{3,1,2,0:T(8,128)} %bitcast.288) | data formatting | bytes 25165824
  97.2 51.0 %rev.9 = f32[6,512,512]{2,1,0:T(8,128)} reverse(f32[6,512,512]{2,1,0:T(8,128)} %slice.37), dimensions={2} | reverse | bytes 12582912 | tf_op jit(solution)/shard_map/rev | solution.py:54
  190.6 16.3 %while.30 = (s32[]{:T(128)}, bf16[2,512,6,64]{1,3,2,0:T(8,128)(2,1)}, f32[2,6,512,1]{2,1,3,0:T(8,128)S(1)}, bf16[2,512,6,64]{1,3,2,0:T(8,128)(2,1)}, s32[2,512]{...) while((s32[]{:T(128)}, ...), condition=%wide.region_8.10_spmd, body=%wide.region_5.9_spmd.sunk | while | flops 417264640 | bytes 36827328 | solution.py:216
  212.7 24.6 %all-reduce.10.cloned.1.call-done = f32[1024,768]{1,0:T(8,128)} async-done(((f32[1024,768]{1,0:T(8,128)}), f32[1024,768]{1,0:T(8,128)}) %all-reduce.10.cloned.1.call-update) | async-done | bytes 3145744 | tf_op jit(solution)/shard_map/psum | solution.py:226
  252.7 24.5 %all-reduce.12.cloned.1.call-done = f32[1024,768]{1,0:T(8,128)} async-done(((f32[1024,768]{1,0:T(8,128)}), f32[1024,768]{1,0:T(8,128)}) %all-reduce.12.cloned.1.call-update) | async-done | bytes 3145744 | tf_op jit(solution)/shard_map/psum | solution.py:232
  289.6 33.3 %all-to-all-done.1 = bf16[1,2,16,32,768]{4,3,1,0,2:T(8,128)(2,1)} async-done(((bf16[1,2,16,32,768]{4,3,1,0,2:T(8,128)(2,1)}), bf16[1,2,16,32,768]{4,3,1,0,2:T(8,128)(2,1)}, u32[]{:S(2)}, u32[]{:S(2)}) %all-to-all-start.1) | async-done | bytes 1572896 | tf_op jit(solution)/shard_map/all_to_all | solution.py:253
  338.0 45.5 %all_to_all.54 = bf16[16,2,32,768]{3,2,1,0:T(8,128)(2,1)S(1)} all-to-all(bf16[16,2,32,768]{3,2,1,0:T(8,128)(2,1)S(1)} %bitcast.296), channel_id=1, replica_groups=mesh['dp'=16,'mp'=2] {'dp'}, dimensions={0} | all-to-all | bytes 3145728 | tf_op jit(solution)/shard_map/all_to_all | solution.py:282
  399.5 18.8 %all-reduce.14.cloned.1.call-done = bf16[1024,768]{1,0:T(8,128)(2,1)} async-done(((bf16[1024,768]{1,0:T(8,128)(2,1)}), bf16[1024,768]{1,0:T(8,128)(2,1)}) %all-reduce.14.cloned.1.call-update) | async-done | bytes 1572880 | tf_op jit(solution)/shard_map/psum | solution.py:312
  431.5 280.4 %while.31 = (s32[]{:T(128)}, bf16[2,512,6,64]{1,3,2,0:T(8,128)(2,1)}, bf16[2,512,6,64]{1,3,2,0:T(8,128)(2,1)}, bf16[2,512,6,64]{1,3,2,0:T(8,128)(2,1)}, f32[2,6,...) while((s32[]{:T(128)}, ...), condition=%wide.region_25.28_spmd, body=%wide.region_22.27_spmd.sunk | while | flops 1028313088 | bytes 306527488 | solution.py:350
  446.5 48.4 %rev.11 = f32[6,512,512]{1,2,0:T(8,128)} reverse(f32[6,512,512]{1,2,0:T(8,128)} %copy-done.2), dimensions={2} | reverse | bytes 12582912 | tf_op jit(solution)/shard_map/while/body/eval_jaxpr/rev | solution.py:59
  510.6 18.0 %copy.201 = f32[1,6,512,1024]{3,1,2,0:T(8,128)} copy(f32[1,6,512,1024]{3,2,1,0:T(8,128)} %pad_bitcast_fusion.2) | data formatting | bytes 25165824 | tf_op jit(solution)/shard_map/while
  539.9 12.2 reshape.493
  552.1 14.0 %reshape.494 = f32[6,512,1023]{2,1,0:T(8,128)} reshape(f32[3142656]{0:T(1024)} %reshape.493) | data formatting | bytes 25141248 | tf_op jit(solution)/shard_map/while/body/eval_jaxpr/reshape | solution.py:61
  586.4 48.4 %rev.11 = f32[6,512,512]{1,2,0:T(8,128)} reverse(f32[6,512,512]{1,2,0:T(8,128)} %copy-done.2), dimensions={2} | reverse | bytes 12582912 | tf_op jit(solution)/shard_map/while/body/eval_jaxpr/rev | solution.py:59
  650.5 18.0 %copy.201 = f32[1,6,512,1024]{3,1,2,0:T(8,128)} copy(f32[1,6,512,1024]{3,2,1,0:T(8,128)} %pad_bitcast_fusion.2) | data formatting | bytes 25165824 | tf_op jit(solution)/shard_map/while
  679.9 12.2 reshape.493
  692.1 14.0 %reshape.494 = f32[6,512,1023]{2,1,0:T(8,128)} reshape(f32[3142656]{0:T(1024)} %reshape.493) | data formatting | bytes 25141248 | tf_op jit(solution)/shard_map/while/body/eval_jaxpr/reshape | solution.py:61
  725.3 18.4 %all-reduce.16.cloned.1.call-done = bf16[1024,768]{1,0:T(8,128)(2,1)} async-done(((bf16[1024,768]{1,0:T(8,128)(2,1)}), bf16[1024,768]{1,0:T(8,128)(2,1)}) %all-reduce.16.cloned.1.call-update) | async-done | bytes 1572880 | tf_op jit(solution)/shard_map/psum | solution.py:369
  780.2 12.3 all-to-all-done.3
  803.4 83.5 %all-reduce.2 = (f32[]{:T(128)}, f32[768]{0:T(1024)}, f32[768]{0:T(1024)}, f32[768]{0:T(1024)}, f32[320,6]{0,1:T(8,128)}, /*index=5*/f32[768]{0:T(1024)}, f32[76...) all-reduce(f32[]{:T(128)S(6)} %add.245, ...), channel_id=1, replica_groups=mesh['dp'=16,'mp'=2] {'dp'}, use_global_device_ids=true, to_apply=%region_18.21 | all-reduce | flops 8226 | bytes 65808 | tf_op jit(solution)/shard_map/psum | solution.py:455
  888.6 379.4 %all-reduce.18.cloned.1.call-done = (f32[512,768]{0,1:T(8,128)}, f32[81,768]{1,0:T(8,128)}, f32[768,384]{1,0:T(8,128)}, f32[768,384]{1,0:T(8,128)}, f32[768,384]...) async-done(((f32[512,768]{0,1:T(8,128)}, f32[81,768]{1,0:T(8,128)}, ...) | async-done | bytes 16472080 | tf_op jit(solution)/shard_map/psum | solution.py:455
  (413 shorter events, 339.1 us)
Async XLA Ops:
  7.2 233.4 %copy-start = (bf16[768,1536]{1,0:T(8,128)(2,1)S(1)}, bf16[768,1536]{1,0:T(8,128)(2,1)}, u32[]{:S(2)}) copy-start(bf16[768,1536]{1,0:T(8,128)(2,1)} %param.54) | copy-start | bytes 7077892
  8.9 317.0 %copy-start.84 = (pred[16]{0:T(512)(128)(4,1)}, pred[16]{0:T(512)(128)(4,1)S(1)}, u32[]{:S(2)}) copy-start(pred[16]{0:T(512)(128)(4,1)S(1)} %get-tuple-element.512) | copy-start | bytes 52
  17.8 138.0 %all-to-all-start = ((bf16[16,2,32,768]{3,2,1,0:T(8,128)(2,1)}), bf16[16,2,32,768]{3,2,1,0:T(8,128)(2,1)}, u32[]{:S(2)}, u32[]{:S(2)}) async-start(bf16[16,2,32,768]{3,2,1,0:T(8,128)(2,1)} %bitcast.294), calls=%async_computation | async-start | bytes 3145728 | tf_op jit(solution)/shard_map/all_to_all | solution.py:186
  26.2 211.1 %all-reduce.10.cloned.1.call-start = ((), (), s32[]{:S(2)}) async-start(), calls=%async_computation.4 | async-start | bytes 6291456 | tf_op jit(solution)/shard_map/psum | solution.py:226
  212.7 64.6 %all-reduce.12.cloned.1.call-start = ((), (), s32[]{:S(2)}) async-start(), calls=%async_computation.5 | async-start | bytes 6291456 | tf_op jit(solution)/shard_map/psum | solution.py:232
  240.0 182.1 %copy-start.69 = (f32[1024]{0:T(1024)}, f32[1024]{0:T(1024)S(1)}, u32[]{:S(2)}) copy-start(f32[1024]{0:T(1024)S(1)} %broadcast_multiply_fusion.5) | copy-start | bytes 12292
  240.8 181.4 %copy-start.71 = (f32[1024]{0:T(1024)}, f32[1024]{0:T(1024)S(1)}, u32[]{:S(2)}) copy-start(f32[1024]{0:T(1024)S(1)} %add_rsqrt_fusion.1) | copy-start | bytes 12292
  252.7 24.6 %copy-start.86 = (f32[768]{0:T(1024)S(1)}, f32[768]{0:T(1024)}, u32[]{:S(2)}) copy-start(f32[768]{0:T(1024)} %param.57) | copy-start | bytes 9220
  281.8 41.2 %all-to-all-start.1 = ((bf16[1,2,16,32,768]{4,3,1,0,2:T(8,128)(2,1)}), bf16[1,2,16,32,768]{4,3,1,0,2:T(8,128)(2,1)}, u32[]{:S(2)}, u32[]{:S(2)}) async-start(bf16[1,2,16,32,768]{4,3,1,0,2:T(8,128)(2,1)} %copy.162), calls=%async_computation.1 | async-start | bytes 3145728 | tf_op jit(solution)/shard_map/all_to_all | solution.py:253
  288.7 39.3 %copy-start.48 = (bf16[768,81]{0,1:T(8,128)(2,1)S(1)}, bf16[768,81]{0,1:T(8,128)(2,1)}, u32[]{:S(2)}) copy-start(bf16[768,81]{0,1:T(8,128)(2,1)} %param.60) | copy-start | bytes 373252
  288.7 129.6 %all-reduce.14.cloned.1.call-start = ((), (), s32[]{:S(2)}) async-start(), calls=%async_computation.6 | async-start | bytes 3145728 | tf_op jit(solution)/shard_map/psum | solution.py:312
  288.9 41.6 %copy-start.60 = (bf16[768,80]{0,1:T(8,128)(2,1)S(1)}, bf16[768,80]{0,1:T(8,128)(2,1)}, u32[]{:S(2)}) copy-start(bf16[768,80]{0,1:T(8,128)(2,1)} %param.58) | copy-start | bytes 368644
  289.6 37.6 %copy-start.83 = (s32[1024]{0:T(1024)}, s32[1024]{0:T(1024)S(1)}, u32[]{:S(2)}) copy-start(s32[1024]{0:T(1024)S(1)} %pad_clamp_fusion) | copy-start | bytes 12292
  337.9 46.8 %copy-start.94 = (bf16[1536,768]{1,0:T(8,128)(2,1)S(1)}, bf16[1536,768]{1,0:T(8,128)(2,1)}, u32[]{:S(2)}) copy-start(bf16[1536,768]{1,0:T(8,128)(2,1)} %param.56) | copy-start | bytes 7077892
  338.0 46.8 %copy-start.98 = (f32[1536]{0:T(1024)S(1)}, f32[1536]{0:T(1024)}, u32[]{:S(2)}) copy-start(f32[1536]{0:T(1024)} %param.55) | copy-start | bytes 18436
  399.4 22.8 %copy-start.17 = (bf16[1,2,16,32,768]{4,3,2,1,0:T(8,128)(2,1)S(1)}, bf16[1,2,16,32,768]{4,3,2,1,0:T(8,128)(2,1)}, u32[]{:S(2)}) copy-start(bf16[1,2,16,32,768]{4,3,2,1,0:T(8,128)(2,1)} %copy-done.16) | copy-start | bytes 4718596
  399.4 344.3 %all-reduce.16.cloned.1.call-start = ((), (), s32[]{:S(2)}) async-start(), calls=%async_computation.7 | async-start | bytes 3145728 | tf_op jit(solution)/shard_map/psum | solution.py:369
  721.9 21.8 %copy-start.64 = (f32[1024]{0:T(1024)S(1)}, f32[1024]{0:T(1024)}, u32[]{:S(2)}) copy-start(f32[1024]{0:T(1024)} %copy-done.63) | copy-start | bytes 12292
  721.9 21.8 %copy-start.66 = (f32[1024]{0:T(1024)S(1)}, f32[1024]{0:T(1024)}, u32[]{:S(2)}) copy-start(f32[1024]{0:T(1024)} %copy-done.65) | copy-start | bytes 12292
  751.2 41.3 %all-to-all-start.3 = ((bf16[1,2,16,32,768]{4,3,1,0,2:T(8,128)(2,1)}), bf16[1,2,16,32,768]{4,3,1,0,2:T(8,128)(2,1)}, u32[]{:S(2)}, u32[]{:S(2)}) async-start(bf16[1,2,16,32,768]{4,3,1,0,2:T(8,128)(2,1)} %copy.174), calls=%async_computation.3 | async-start | bytes 3145728 | tf_op jit(solution)/shard_map/all_to_all | solution.py:401
  758.2 509.8 %all-reduce.18.cloned.1.call-start = ((), (), s32[]{:S(2)}) async-start(), calls=%async_computation.8 | async-start | bytes 33030144 | tf_op jit(solution)/shard_map/psum | solution.py:455
  778.4 16.3 %copy-start.85 = (pred[16]{0:T(512)(128)(4,1)S(1)}, pred[16]{0:T(512)(128)(4,1)}, u32[]{:S(2)}) copy-start(pred[16]{0:T(512)(128)(4,1)} %copy-done.84) | copy-start | bytes 52
  780.2 14.7 %copy-start.95 = (bf16[8,32,512]{2,1,0:T(8,128)(2,1)S(1)}, bf16[8,32,512]{2,1,0:T(8,128)(2,1)}, u32[]{:S(2)}) copy-start(bf16[8,32,512]{2,1,0:T(8,128)(2,1)} %param.35) | copy-start | bytes 786436
  797.4 90.0 %copy-start.42 = (bf16[512,768]{1,0:T(8,128)(2,1)S(1)}, bf16[512,768]{1,0:T(8,128)(2,1)}, u32[]{:S(2)}) copy-start(bf16[512,768]{1,0:T(8,128)(2,1)} %param.42) | copy-start | bytes 2359300
  (99 other events, 399.1 us)
Sparse Core Ops, SparseCore 0:
  212.8 24.4 all-reduce.9
  252.8 24.3 all-reduce.11
  399.5 18.7 all-reduce.13
  722.1 21.5 all-reduce.15
  797.6 470.3 all-reduce.17
where the time goes:
time: 1310 us; the launch traced here: 1290 us
  waiting for transfers between devices  511 us (39%)
  local copies, waits for them, and re-layouts  445 us (34%)
  blocking collectives  129 us (10%)
  matrix products  101 us (8%)
  other arithmetic  64.5 us (5%)
  starting transfers between devices  22.4 us (2%)
  between operations  18.3 us (1%)
    psum x1, waiting for transfers between devices, per_device(): lax.psum((grad_down, grad_down_bias, grad_up, grad_up_bias, grad_second_g...  379 us
    rev x2, local copies, waits for them, and re-layouts, diagonal_sums(): score_grid[:, :, ::-1]  96.8 us
    while x40, local copies, waits for them, and re-layouts  96 us
    psum x1, blocking collectives, per_device(): lax.psum((grad_down, grad_down_bias, grad_up, grad_up_bias, grad_second_g...  83.5 us
    unnamed x214, local copies, waits for them, and re-layouts  58.8 us
    rev x1, local copies, waits for them, and re-layouts, toeplitz(): widened.reshape(head_count, length, 2 * length)[:, :, :length][:, :, ::-1]  51 us
    all_to_all x1, blocking collectives, per_device(): lax.all_to_all(to_slots(grad_rows, row_of_slot, slot_used, devices, capac...  45.5 us
    all_to_all x1, waiting for transfers between devices, per_device(): lax.all_to_all(for_return(final_low, devices), 'dp', split_axis=2, concat...  33.3 us
  transfers between devices with their start and end apart: 8, of which 7 were waited for; matrix products, arithmetic and copies ran while one was open for 12% of the time, Pallas kernels for 0%

commit v1 on v0

v1 whole, which is shorter than its diff:
```python
import jax
import jax.numpy as jnp
from jax import lax
from jax.experimental import pallas as pl
from jax.experimental.pallas import tpu as pltpu
from jax.sharding import PartitionSpec as P

EPSILON = 1e-05
NEGATIVE = -1e30
HIGHEST = lax.Precision.HIGHEST
BF16 = jnp.bfloat16
F32 = jnp.float32
LANES = 128


def contract_rows(left_side, right_side):
    return lax.dot_general(
        left_side, right_side, (((0,), (0,)), ((), ())), preferred_element_type=F32
    )


def times_transposed(left_side, right_side):
    return lax.dot_general(
        left_side, right_side, (((1,), (1,)), ((), ())), preferred_element_type=F32
    )


def matmul(left_side, right_side):
    return jnp.dot(left_side, right_side, preferred_element_type=F32)


def layer_norm(row_data, norm_gain, norm_shift):
    center = row_data - jnp.mean(row_data, axis=-1, keepdims=True)
    inverse = lax.rsqrt(jnp.mean(center * center, axis=-1, keepdims=True) + EPSILON)
    normal = center * inverse
    return (normal * norm_gain + norm_shift, normal, inverse)


def norm_back(grad_out, normal, inverse, norm_gain):
    scaled = grad_out * norm_gain
    grad_rows = inverse * (
        scaled
        - jnp.mean(scaled, axis=-1, keepdims=True)
        - normal * jnp.mean(scaled * normal, axis=-1, keepdims=True)
    )
    return (grad_rows, jnp.sum(grad_out * normal, axis=0), jnp.sum(grad_out, axis=0))


def smooth_gelu(hidden):
    return jax.nn.gelu(hidden, approximate=True)


def window_kernel(offsets_ref, window_ref):
    heads, width = offsets_ref.shape
    for head in range(heads):
        spread = jnp.broadcast_to(offsets_ref[head : head + 1, :], (LANES, width))
        window_ref[head] = pltpu.roll(spread, width - LANES + 1, 1, stride=1, stride_axis=0)


def bias_window(offsets):
    heads, width = offsets.shape
    return pl.pallas_call(
        window_kernel,
        out_shape=jax.ShapeDtypeStruct((heads, LANES, width), F32),
        name="bias_window",
    )(offsets)


def block_probs(queries, keys, window_ref, slot, block, blocks, segment_column, segment_row):
    length = keys.shape[0]
    start = LANES * (blocks - 1 - block)
    scores = times_transposed(queries, keys) + window_ref[slot, :, start : start + length]
    scores = jnp.where(segment_column == segment_row, scores, NEGATIVE)
    powers = jnp.exp(scores - jnp.max(scores, axis=-1, keepdims=True))
    return powers * (1.0 / jnp.sum(powers, axis=-1, keepdims=True))


def attend_kernel(
    head_size, queries_ref, keys_ref, values_ref, column_ref, row_ref, window_ref, heads_ref
):
    length = queries_ref.shape[0]
    blocks = length // LANES
    scaling = head_size ** (-0.5)
    for slot in range(queries_ref.shape[1] // head_size):
        columns = slice(slot * head_size, (slot + 1) * head_size)
        keys = keys_ref[:, columns]
        values = values_ref[:, columns]
        for block in range(blocks):
            rows = slice(block * LANES, (block + 1) * LANES)
            queries = queries_ref[rows, columns] * jnp.asarray(scaling, BF16)
            probs = block_probs(
                queries, keys, window_ref, slot, block, blocks, column_ref[rows, :], row_ref[...]
            )
            heads_ref[rows, columns] = matmul(probs.astype(BF16), values).astype(BF16)


def attend(queries, keys, values, segment_column, segment_row, window, head_size):
    length, width = queries.shape
    per_step = LANES // head_size
    flat = pl.BlockSpec((length, LANES), lambda step: (0, step))
    return pl.pallas_call(
        lambda *refs: attend_kernel(head_size, *refs),
        grid=(width // LANES,),
        in_specs=[
            flat,
            flat,
            flat,
            pl.BlockSpec((length, 1), lambda step: (0, 0)),
            pl.BlockSpec((1, length), lambda step: (0, 0)),
            pl.BlockSpec((per_step, LANES, 2 * length), lambda step: (step, 0, 0)),
        ],
        out_specs=flat,
        out_shape=jax.ShapeDtypeStruct((length, width), BF16),
        name="attend",
    )(queries, keys, values, segment_column, segment_row, window)


def attend_back_kernel(
    head_size,
    queries_ref,
    keys_ref,
    values_ref,
    grads_ref,
    column_ref,
    row_ref,
    window_ref,
    grad_queries_ref,
    grad_keys_ref,
    grad_values_ref,
    grad_offsets_ref,
    probs_ref,
    scores_ref,
    window_sum_ref,
):
    length = queries_ref.shape[0]
    blocks = length // LANES
    scaling = head_size ** (-0.5)
    for slot in range(queries_ref.shape[1] // head_size):
        columns = slice(slot * head_size, (slot + 1) * head_size)
        keys = keys_ref[:, columns]
        values = values_ref[:, columns]
        window_sum_ref[...] = jnp.zeros_like(window_sum_ref)
        for block in range(blocks):
            rows = slice(block * LANES, (block + 1) * LANES)
            queries = queries_ref[rows, columns] * jnp.asarray(scaling, BF16)
            probs = block_probs(
                queries, keys, window_ref, slot, block, blocks, column_ref[rows, :], row_ref[...]
            )
            grad_probs = times_transposed(grads_ref[rows, columns], values)
            grad_scores = probs * (
                grad_probs - jnp.sum(probs * grad_probs, axis=-1, keepdims=True)
            )
            probs_ref[rows, :] = probs.astype(BF16)
            scores_ref[rows, :] = grad_scores.astype(BF16)
            start = LANES * (blocks - 1 - block)
            window_sum_ref[:, start : start + length] += grad_scores
        grad_queries_ref[:, columns] = (matmul(scores_ref[...], keys) * scaling).astype(BF16)
        grad_keys_ref[:, columns] = (
            contract_rows(scores_ref[...], queries_ref[:, columns]) * scaling
        ).astype(BF16)
        grad_values_ref[:, columns] = contract_rows(probs_ref[...], grads_ref[:, columns]).astype(
            BF16
        )
        diagonal = window_sum_ref[...]
        half = LANES // 2
        while half >= 1:
            diagonal = pltpu.roll(diagonal[:half], half, 1) + diagonal[half:]
            half //= 2
        grad_offsets_ref[0, slot : slot + 1, :] = diagonal


def attend_back(queries, keys, values, grads, segment_column, segment_row, window, head_size):
    length, width = queries.shape
    per_step = LANES // head_size
    steps = width // LANES
    flat = pl.BlockSpec((length, LANES), lambda step: (0, step))
    flat_shape = jax.ShapeDtypeStruct((length, width), BF16)
    grad_queries, grad_keys, grad_values, grad_offsets = pl.pallas_call(
        lambda *refs: attend_back_kernel(head_size, *refs),
        grid=(steps,),
        in_specs=[
            flat,
            flat,
            flat,
            flat,
            pl.BlockSpec((length, 1), lambda step: (0, 0)),
            pl.BlockSpec((1, length), lambda step: (0, 0)),
            pl.BlockSpec((per_step, LANES, 2 * length), lambda step: (step, 0, 0)),
        ],
        out_specs=[
            flat,
            flat,
            flat,
            pl.BlockSpec((1, per_step, 2 * length), lambda step: (step, 0, 0)),
        ],
        out_shape=[
            flat_shape,
            flat_shape,
            flat_shape,
            jax.ShapeDtypeStruct((steps, per_step, 2 * length), F32),
        ],
        scratch_shapes=[
            pltpu.VMEM((length, length), BF16),
            pltpu.VMEM((length, length), BF16),
            pltpu.VMEM((LANES, 2 * length), F32),
        ],
        name="attend_back",
    )(queries, keys, values, grads, segment_column, segment_row, window)
    return grad_queries, grad_keys, grad_values, grad_offsets.reshape(steps * per_step, 2 * length)


def swap_cores(array):
    return lax.ppermute(array, "mp", [(0, 1), (1, 0)])


def add_small(values, devices):
    sizes = [value.size for value in values]
    flat = jnp.concatenate([value.reshape(-1) for value in values])
    rows = -(-flat.size // (8 * LANES)) * 8
    flat = jnp.pad(flat, (0, rows * LANES - flat.size)).reshape(rows, LANES)
    step = 1
    while step < devices:
        flat = flat + lax.ppermute(flat, "dp", [(i, i ^ step) for i in range(devices)])
        step *= 2
    flat = flat.reshape(-1)
    summed = []
    start = 0
    for value, size in zip(values, sizes):
        summed.append(flat[start : start + size].reshape(value.shape))
        start += size
    return summed


def add_large(values):
    return [
        value.astype(F32) for value in lax.psum([value.astype(BF16) for value in values], "dp")
    ]


def per_device(
    features,
    token_ids,
    mel_target,
    token_target,
    segments,
    row_device,
    offset_bucket,
    speech_weight,
    speech_bias,
    token_table,
    first_gain,
    first_shift,
    query_weight,
    key_weight,
    value_weight,
    bias_table,
    out_weight,
    second_gain,
    second_shift,
    up_weight,
    up_bias,
    down_weight,
    down_bias,
    mel_weight,
    mel_bias,
    vocab_weight,
    vocab_bias,
):
    devices = lax.axis_size("dp")
    device_index = lax.axis_index("dp")
    rows_speech, part_len, feat_width = features.shape
    rows_text = token_ids.shape[0]
    rows_total, length = segments.shape
    vocab_size = token_table.shape[0]
    mel_width = mel_weight.shape[1]
    local_heads = bias_table.shape[1]
    head_size = query_weight.shape[1] // local_heads
    is_speech = device_index < rows_speech

    plain_width = feat_width + mel_width
    sent_width = -(-(plain_width + 2) // LANES) * LANES
    speech_part = jnp.concatenate(
        [features, mel_target, jnp.zeros((rows_speech, part_len, sent_width - plain_width), BF16)],
        axis=2,
    )
    text_part = jnp.concatenate(
        [
            jnp.zeros((rows_text, part_len, plain_width), BF16),
            token_ids[:, :, None].astype(BF16),
            token_target[:, :, None].astype(BF16),
            jnp.zeros((rows_text, part_len, sent_width - plain_width - 2), BF16),
        ],
        axis=2,
    )
    arrived = lax.all_to_all(
        jnp.concatenate([speech_part, text_part], axis=0),
        "dp",
        split_axis=0,
        concat_axis=0,
        tiled=True,
    ).reshape(length, sent_width)
    my_features = arrived[:, :feat_width]
    my_mel = arrived[:, feat_width:plain_width]
    my_ids = arrived[:, plain_width].astype(jnp.int32)
    my_labels = arrived[:, plain_width + 1].astype(jnp.int32)

    my_segments = lax.dynamic_slice_in_dim(segments, device_index, 1)
    segment_column = my_segments.reshape(length, 1)
    reversed_bucket = jnp.pad(offset_bucket[::-1], (0, 1), constant_values=-1)
    bucket_hot = (reversed_bucket[:, None] == jnp.arange(bias_table.shape[0])[None, :]).astype(F32)
    offsets = jnp.dot(bucket_hot, bias_table, precision=HIGHEST).T
    window = bias_window(offsets)

    hot_ids = ((my_ids[:, None] == jnp.arange(vocab_size)[None, :]) & ~is_speech).astype(BF16)
    embedded = (
        matmul(my_features, speech_weight)
        + matmul(hot_ids, token_table)
        + jnp.where(is_speech, speech_bias, 0.0)
    ).astype(BF16)
    flat_rows = embedded.astype(F32)
    norm_one, normal_one, inverse_one = layer_norm(flat_rows, first_gain, first_shift)
    norm_one_low = norm_one.astype(BF16)
    queries = matmul(norm_one_low, query_weight).astype(BF16)
    key_rows = matmul(norm_one_low, key_weight).astype(BF16)
    value_rows = matmul(norm_one_low, value_weight).astype(BF16)
    heads_flat = attend(
        queries, key_rows, value_rows, segment_column, my_segments, window, head_size
    )
    attended = matmul(heads_flat, out_weight)
    mixed_rows = flat_rows + (attended + swap_cores(attended))
    norm_two, normal_two, inverse_two = layer_norm(mixed_rows, second_gain, second_shift)
    norm_two_low = norm_two.astype(BF16)
    hidden = matmul(norm_two_low, up_weight) + up_bias
    active_low = smooth_gelu(hidden).astype(BF16)
    branch = matmul(active_low, down_weight)
    final_low = (mixed_rows + (branch + swap_cores(branch)) + down_bias).astype(BF16)

    predicted = matmul(final_low, mel_weight) + mel_bias
    mel_error = predicted - my_mel.astype(F32)
    smooth = jnp.sqrt(mel_error * mel_error + 1.0)
    mel_scale = jnp.where(is_speech, 1.0 / (mel_width * length), 0.0)
    mel_sum = jnp.sum((smooth - 1.0) * mel_scale)
    grad_predicted = (mel_error / smooth * mel_scale).astype(BF16)
    logits = matmul(final_low, vocab_weight) + vocab_bias
    shifted = logits - jnp.max(logits, axis=-1, keepdims=True)
    powers = jnp.exp(shifted)
    totals = jnp.sum(powers, axis=-1, keepdims=True)
    label_hot = (my_labels[:, None] == jnp.arange(vocab_size)[None, :]).astype(F32)
    text_scale = jnp.where(is_speech, 0.0, 1.0 / length)
    losses = jnp.log(totals) - jnp.sum(shifted * label_hot, axis=-1, keepdims=True)
    text_sum = jnp.sum(losses * text_scale)
    grad_logits = ((powers / totals - label_hot) * text_scale).astype(BF16)
    local_loss = mel_sum + text_sum
    grad_mel_weight = contract_rows(final_low, grad_predicted)
    grad_mel_bias = jnp.sum(grad_predicted.astype(F32), axis=0)
    grad_vocab_weight = contract_rows(final_low, grad_logits)
    grad_vocab_bias = jnp.sum(grad_logits.astype(F32), axis=0)
    grad_final = (
        times_transposed(grad_predicted, mel_weight) + times_transposed(grad_logits, vocab_weight)
    ).astype(BF16)

    grad_down = contract_rows(active_low, grad_final)
    grad_down_bias = jnp.sum(grad_final.astype(F32), axis=0)
    grad_active = times_transposed(grad_final, down_weight)
    gelu_back = jax.vjp(smooth_gelu, hidden)[1]
    grad_hidden_low = gelu_back(grad_active)[0].astype(BF16)
    grad_up = contract_rows(norm_two_low, grad_hidden_low)
    grad_up_bias = jnp.sum(grad_hidden_low.astype(F32), axis=0)
    grad_down, grad_up, grad_mel_weight, grad_vocab_weight = add_large(
        [grad_down, grad_up, grad_mel_weight, grad_vocab_weight]
    )
    grad_norm_two = times_transposed(grad_hidden_low, up_weight).astype(BF16)
    grad_norm_two = grad_norm_two.astype(F32) + swap_cores(grad_norm_two).astype(F32)
    grad_mixed_part, grad_second_gain, grad_second_shift = norm_back(
        grad_norm_two, normal_two, inverse_two, second_gain
    )
    grad_mixed = grad_final.astype(F32) + grad_mixed_part
    grad_mixed_low = grad_mixed.astype(BF16)
    grad_out = contract_rows(heads_flat, grad_mixed_low)
    grad_heads = times_transposed(grad_mixed_low, out_weight).astype(BF16)
    grad_queries, grad_keys, grad_values, grad_offsets = attend_back(
        queries, key_rows, value_rows, grad_heads, segment_column, my_segments, window, head_size
    )
    grad_table = jnp.dot(bucket_hot.T, grad_offsets.T, precision=HIGHEST)
    grad_query = contract_rows(norm_one_low, grad_queries)
    grad_key = contract_rows(norm_one_low, grad_keys)
    grad_value = contract_rows(norm_one_low, grad_values)
    grad_norm_one = (
        times_transposed(grad_queries, query_weight)
        + times_transposed(grad_keys, key_weight)
        + times_transposed(grad_values, value_weight)
    ).astype(BF16)
    grad_norm_one = grad_norm_one.astype(F32) + swap_cores(grad_norm_one).astype(F32)
    grad_in_part, grad_first_gain, grad_first_shift = norm_back(
        grad_norm_one, normal_one, inverse_one, first_gain
    )
    grad_embedded = (grad_mixed + grad_in_part).astype(BF16)
    grad_speech_weight = contract_rows(my_features, grad_embedded)
    grad_speech_bias = jnp.where(is_speech, jnp.sum(grad_embedded.astype(F32), axis=0), 0.0)
    grad_token_table = contract_rows(hot_ids, grad_embedded)
    feature_back = times_transposed(grad_embedded, speech_weight).astype(BF16)
    feature_grad = lax.all_to_all(
        feature_back.reshape(devices, part_len, feat_width),
        "dp",
        split_axis=0,
        concat_axis=0,
        tiled=True,
    )[:rows_speech]
    (grad_out, grad_query, grad_key, grad_value, grad_speech_weight, grad_token_table) = add_large(
        [grad_out, grad_query, grad_key, grad_value, grad_speech_weight, grad_token_table]
    )
    (
        loss_total,
        grad_down_bias,
        grad_up_bias,
        grad_second_gain,
        grad_second_shift,
        grad_mel_bias,
        grad_vocab_bias,
        grad_table,
        grad_first_gain,
        grad_first_shift,
        grad_speech_bias,
    ) = add_small(
        [
            local_loss,
            grad_down_bias,
            grad_up_bias,
            grad_second_gain,
            grad_second_shift,
            grad_mel_bias,
            grad_vocab_bias,
            grad_table,
            grad_first_gain,
            grad_first_shift,
            grad_speech_bias,
        ],
        devices,
    )
    return (
        loss_total / rows_total,
        feature_grad,
        grad_speech_weight,
        grad_speech_bias,
        grad_token_table,
        grad_first_gain,
        grad_first_shift,
        grad_query,
        grad_key,
        grad_value,
        grad_table,
        grad_out,
        grad_second_gain,
        grad_second_shift,
        grad_up,
        grad_up_bias,
        grad_down,
        grad_down_bias,
        grad_mel_weight,
        grad_mel_bias,
        grad_vocab_weight,
        grad_vocab_bias,
    )


def solution(mesh):
    placed = (
        P(None, "dp", None),
        P(None, "dp"),
        P(None, "dp", None),
        P(None, "dp"),
        P(),
        P(),
        P(),
        P(),
        P(),
        P(),
        P(),
        P(),
        P(None, "mp"),
        P(None, "mp"),
        P(None, "mp"),
        P(None, "mp"),
        P("mp", None),
        P(),
        P(),
        P(None, "mp"),
        P("mp"),
        P("mp", None),
        P(),
        P(),
        P(),
        P(),
        P(),
    )
    return jax.shard_map(
        per_device,
        mesh=mesh,
        in_specs=placed,
        out_specs=(
            P(),
            P(None, "dp", None),
            P(),
            P(),
            P(),
            P(),
            P(),
            P(None, "mp"),
            P(None, "mp"),
            P(None, "mp"),
            P(None, "mp"),
            P("mp", None),
            P(),
            P(),
            P(None, "mp"),
            P("mp"),
            P("mp", None),
            P(),
            P(),
            P(),
            P(),
            P(),
        ),
        check_vma=False,
    )
```

time: 1310 us -> 423 us (0.32); the launches traced: 1290 us -> 422 us
  local copies, waits for them, and re-layouts: 445 us -> 14.7 us
  waiting for transfers between devices: 511 us -> 266 us
  blocking collectives: 129 us -> 0 us
  matrix products: 101 us -> 43.8 us
  other arithmetic: 64.5 us -> 27 us
  Pallas kernels: 0 us -> 29 us
    psum x5 -> x1, waiting for transfers between devices: 466 us -> 229 us  [add_large(): lax.psum([value.astype(BF16) for value in values], 'dp')]
    rev x3 -> x0, local copies, waits for them, and re-layouts: 148 us -> none  [the longest x2 96.8 us: diagonal_sums(): score_grid[:, :, ::-1]]
    while x49 -> x0, local copies, waits for them, and re-layouts: 116 us -> none
    psum x1 -> x0, blocking collectives: 83.5 us -> none  [per_device(): lax.psum((grad_down, grad_down_bias, grad_up, grad_up_bias, grad_second_g...]
    unnamed x214 -> x106, local copies, waits for them, and re-layouts: 58.8 us -> 5.68 us
    reshape x7 -> x5, local copies, waits for them, and re-layouts: 50.5 us -> 1.75 us  [the longest x2 1.59 us: per_device(): segment_column = my_segments.reshape(length, 1)]
    all_to_all x1 -> x0, blocking collectives: 45.5 us -> none  [per_device(): lax.all_to_all(to_slots(grad_rows, row_of_slot, slot_used, devices, capac...]
    dot_general x25 -> x11, matrix products: 55.5 us -> 15.4 us  [the longest x10 13.9 us: matmul(): return jnp.dot(left_side, right_side, preferred_element_type=F32)]
  transfers between devices with their start and end apart: 8 -> 11, of which waited for: 7 -> 8; matrix products, arithmetic and copies ran while one was open for 12% -> 6% of each run, Pallas kernels for 0% -> 1%
where the time goes in v1:
time: 423 us; the launch traced here: 422 us
  waiting for transfers between devices  266 us (63%)
  matrix products  43.8 us (10%)
  Pallas kernels  29 us (7%)
  other arithmetic  27 us (6%)
  starting transfers between devices  24 us (6%)
  between operations  17.8 us (4%)
  local copies, waits for them, and re-layouts  14.7 us (3%)
    psum x1, waiting for transfers between devices, add_large(): lax.psum([value.astype(BF16) for value in values], 'dp')  229 us
    ppermute x4, waiting for transfers between devices, add_small(): lax.ppermute(flat, 'dp', [(i, i ^ step) for i in range(devices)])  21.6 us
    dot_general x10, matrix products, contract_rows(): lax.dot_general(left_side, right_side, (((0,), (0,)), ((), ())), preferre...  16.1 us
    convert_element_type x10, other arithmetic, add_large(): value.astype(F32)  15 us
    pallas_call x1, Pallas kernels, attend_back(): pl.pallas_call(lambda *refs: attend_back_kernel(head_size, *refs), grid=(...  14.2 us
    dot_general x10, matrix products, matmul(): return jnp.dot(left_side, right_side, preferred_element_type=F32)  13.9 us
    pallas_call x1, Pallas kernels, attend(): pl.pallas_call(lambda *refs: attend_kernel(head_size, *refs), grid=(width...  11.4 us
    dot_general x9, matrix products, times_transposed(): lax.dot_general(left_side, right_side, (((1,), (1,)), ((), ())), preferre...  11.1 us
  transfers between devices with their start and end apart: 11, of which 8 were waited for; matrix products, arithmetic and copies ran while one was open for 6% of the time, Pallas kernels for 1%

profile of v1, /device:TPU:0, one launch (start us, length us, event | category | flops | bytes accessed | tf_op | source)
XLA Modules:
  0.0 421.9 jit_solution(12710557844607685812)
XLA Ops:
  9.2 2.0 maximum_maximum_fusion
  11.3 8.3 %all-to-all-start = ((bf16[16,32,640]{2,1,0:T(8,128)(2,1)}), bf16[16,32,640]{2,1,0:T(8,128)(2,1)S(1)}, u32[]{:S(2)}, u32[]{:S(2)}) async-start(bf16[16,32,640]{2,1,0:T(8,128)(2,1)} %maximum_maximum_fusion), calls=%async_computation | async-start | bytes 1310720 | tf_op jit(solution)/shard_map/all_to_all | solution.py:295
  22.9 3.3 bias_window.1.refs_5_.refs_6_
  27.6 9.5 %all-to-all-done = bf16[16,32,640]{2,1,0:T(8,128)(2,1)S(1)} async-done(((bf16[16,32,640]{2,1,0:T(8,128)(2,1)}), bf16[16,32,640]{2,1,0:T(8,128)(2,1)S(1)}, u32[]{:S(2)}, u32[]{:S(2)}) %all-to-all-start) | async-done | bytes 655392 | tf_op jit(solution)/shard_map/all_to_all | solution.py:295
  45.2 11.4 %attend.1 = bf16[512,384]{1,0:T(8,128)(2,1)} custom-call(bf16[512,384]{1,0:T(8,128)(2,1)} %convolution_convert_fusion.12.refs_0_, bf16[512,384]{1,0:T(8,128)(2,1)} %convolution_convert_fusion.11.refs_1_, bf16[512,384]{1,0:T(8,128)(2,1)} %convolution_convert_fusion.10.refs_2_, s32[512,1]{1,0:T(8,128)} %copy.58.refs_3_.refs_4_, ...), custom_call_target="tpu_custom_call" | custom-call | tf_op jit(solution)/shard_map/attend/pallas_call | solution.py:101
  58.4 3.4 collective-permute-done
  65.6 3.1 fusion.49
  69.9 2.6 collective-permute-done.1
  72.4 2.7 add_convert_fusion.2
  78.5 3.4 convert_reduce_fusion
  81.9 3.0 convolution_convert_fusion.1
  88.4 3.2 convolution_convert_fusion
  94.9 14.2 %attend_back.1 = (bf16[512,384]{1,0:T(8,128)(2,1)}, bf16[512,384]{1,0:T(8,128)(2,1)}, bf16[512,384]{1,0:T(8,128)(2,1)}, f32[3,2,1024]{2,1,0:T(2,128)}) custom-call(bf16[512,384]{1,0:T(8,128)(2,1)} %convolution_convert_fusion.12.refs_0_, bf16[512,384]{1,0:T(8,128)(2,1)} %convolution_convert_fusion.11.refs_1_, ...), custom_call_target="tpu_custom_call" | custom-call | tf_op jit(solution)/shard_map/attend_back/pallas_call | solution.py:178
  127.9 4.4 %all-to-all-start.1 = ((bf16[16,32,512]{2,1,0:T(8,128)(2,1)}), bf16[16,32,512]{2,1,0:T(8,128)(2,1)S(1)}, u32[]{:S(2)}, u32[]{:S(2)}) async-start(bf16[16,32,512]{2,1,0:T(8,128)(2,1)} %bitcast.9), calls=%async_computation.1 | async-start | bytes 1048576 | tf_op jit(solution)/shard_map/all_to_all | solution.py:402
  132.4 2.0 collective-permute-start.4
  134.4 5.5 %collective-permute-done.4 = f32[72,128]{1,0:T(8,128)S(1)} collective-permute-done((f32[72,128]{1,0:T(8,128)S(1)}, f32[72,128]{1,0:T(8,128)S(1)}, u32[]{:S(2)}, u32[]{:S(2)}) %collective-permute-start.4) | collective-permute-done | bytes 36896 | tf_op jit(solution)/shard_map/ppermute | solution.py:223
  141.4 3.3 collective-permute-done.5
  144.7 2.2 collective-permute-start.6
  146.9 4.7 %collective-permute-done.6 = f32[72,128]{1,0:T(8,128)S(1)} collective-permute-done((f32[72,128]{1,0:T(8,128)S(1)}, f32[72,128]{1,0:T(8,128)S(1)}, u32[]{:S(2)}, u32[]{:S(2)}) %collective-permute-start.6) | collective-permute-done | bytes 36896 | tf_op jit(solution)/shard_map/ppermute | solution.py:223
  151.6 4.7 %collective-permute-start.7 = (f32[72,128]{1,0:T(8,128)S(1)}, f32[72,128]{1,0:T(8,128)S(1)}, u32[]{:S(2)}, u32[]{:S(2)}) collective-permute-start(f32[72,128]{1,0:T(8,128)S(1)} %add.198), channel_id=1, source_target_pairs={{0,16},{2,18},{4,20},{6,22},{8,24},{10,26},{12,28},{14,30},{16,0},... | collective-permute-start | bytes 110600 | tf_op jit(solution)/shard_map/ppermute | solution.py:223
  156.4 8.1 %collective-permute-done.7 = f32[72,128]{1,0:T(8,128)S(1)} collective-permute-done((f32[72,128]{1,0:T(8,128)S(1)}, f32[72,128]{1,0:T(8,128)S(1)}, u32[]{:S(2)}, u32[]{:S(2)}) %collective-permute-start.7) | collective-permute-done | bytes 36896 | tf_op jit(solution)/shard_map/ppermute | solution.py:223
  170.3 228.6 %all-reduce.5.cloned.1.call-done = (bf16[512,768]{1,0:T(8,128)(2,1)}, bf16[81,768]{1,0:T(8,128)(2,1)}, bf16[768,384]{1,0:T(8,128)(2,1)}, bf16[768,384]{1,0:T(8,1...) async-done(((bf16[512,768]{1,0:T(8,128)(2,1)}, ...) | async-done | bytes 8236048 | tf_op jit(solution)/shard_map/psum | solution.py:236
  398.9 4.6 %convert_element_type.218 = f32[768,1536]{1,0:T(8,128)} convert(bf16[768,1536]{1,0:T(8,128)(2,1)} %get-tuple-element.92) | non-fusion elementwise | flops 1179648 | bytes 7077888 | tf_op jit(solution)/shard_map/convert_element_type | solution.py:236
  403.6 2.5 convert_element_type.220
  (203 shorter events, 63.4 us)
Async XLA Ops:
  7.2 58.3 %copy-start = (bf16[1536,768]{1,0:T(8,128)(2,1)S(1)}, bf16[1536,768]{1,0:T(8,128)(2,1)}, u32[]{:S(2)}) copy-start(bf16[1536,768]{1,0:T(8,128)(2,1)} %param.47) | copy-start | bytes 7077892
  7.2 14.0 %copy-start.38 = (s32[1023]{0:T(1024)S(1)}, s32[1023]{0:T(1024)}, u32[]{:S(2)}) copy-start(s32[1023]{0:T(1024)} %param.32) | copy-start | bytes 12280
  7.2 14.2 %copy-start.45 = (f32[320,6]{0,1:T(8,128)S(1)}, f32[320,6]{0,1:T(8,128)}, u32[]{:S(2)}) copy-start(f32[320,6]{0,1:T(8,128)} %param.41) | copy-start | bytes 23044
  11.3 25.7 %all-to-all-start = ((bf16[16,32,640]{2,1,0:T(8,128)(2,1)}), bf16[16,32,640]{2,1,0:T(8,128)(2,1)S(1)}, u32[]{:S(2)}, u32[]{:S(2)}) async-start(bf16[16,32,640]{2,1,0:T(8,128)(2,1)} %maximum_maximum_fusion), calls=%async_computation | async-start | bytes 1310720 | tf_op jit(solution)/shard_map/all_to_all | solution.py:295
  19.6 379.3 %all-reduce.5.cloned.1.call-start = ((), (), s32[]{:S(2)}) async-start(), calls=%async_computation.2 | async-start | bytes 16515072 | tf_op jit(solution)/shard_map/psum | solution.py:236
  22.9 4.6 %copy-start.39 = (f32[768]{0:T(1024)S(1)}, f32[768]{0:T(1024)}, u32[]{:S(2)}) copy-start(f32[768]{0:T(1024)} %param.34) | copy-start | bytes 9220
  22.9 14.9 %copy-start.28 = (bf16[81,768]{1,0:T(8,128)(2,1)S(1)}, bf16[81,768]{1,0:T(8,128)(2,1)}, u32[]{:S(2)}) copy-start(bf16[81,768]{1,0:T(8,128)(2,1)} %param.35) | copy-start | bytes 373252
  58.3 3.5 collective-permute-start
  62.1 3.4 copy-start.2
  65.5 6.9 %copy-start.37 = (f32[768]{0:T(1024)S(1)}, f32[768]{0:T(1024)}, u32[]{:S(2)}) copy-start(f32[768]{0:T(1024)} %param.48) | copy-start | bytes 9220
  68.7 3.8 collective-permute-start.1
  69.8 5.3 %copy-start.31 = (bf16[768,80]{0,1:T(8,128)(2,1)S(1)}, bf16[768,80]{0,1:T(8,128)(2,1)}, u32[]{:S(2)}) copy-start(bf16[768,80]{0,1:T(8,128)(2,1)} %param.49) | copy-start | bytes 368644
  69.8 5.3 %copy-start.48 = (f32[80]{0:T(128)S(1)}, f32[80]{0:T(128)}, u32[]{:S(2)}) copy-start(f32[80]{0:T(128)} %param.50) | copy-start | bytes 964
  78.5 3.4 copy-start.3
  86.4 5.2 %collective-permute-start.2 = (bf16[512,768]{1,0:T(8,128)(2,1)S(1)}, bf16[512,768]{1,0:T(8,128)(2,1)S(1)}, u32[]{:S(2)}, u32[]{:S(2)}) collective-permute-start(bf16[512,768]{1,0:T(8,128)(2,1)S(1)} %convolution_convert_fusion.3), channel_id=1, source_target_pairs={{0,1},{1,0},{2,3},{3,2},{4,5},{5,4},{6,7},{7,6},{8,9},{9,8},{10,11... | collective-permute-start | bytes 2359304 | tf_op jit(solution)/shard_map/ppermute | solution.py:213
  94.9 14.3 %copy-start.17 = (bf16[768,384]{1,0:T(8,128)(2,1)S(1)}, bf16[768,384]{1,0:T(8,128)(2,1)}, u32[]{:S(2)}) copy-start(bf16[768,384]{1,0:T(8,128)(2,1)} %param.38) | copy-start | bytes 1769476
  114.1 4.6 %collective-permute-start.3 = (bf16[512,768]{1,0:T(8,128)(2,1)S(1)}, bf16[512,768]{1,0:T(8,128)(2,1)S(1)}, u32[]{:S(2)}, u32[]{:S(2)}) collective-permute-start(bf16[512,768]{1,0:T(8,128)(2,1)S(1)} %add_convert_fusion), channel_id=1, source_target_pairs={{0,1},{1,0},{2,3},{3,2},{4,5},{5,4},{6,7},{7,6},{8,9},{9,8},{10,11... | collective-permute-start | bytes 2359304 | tf_op jit(solution)/shard_map/ppermute | solution.py:213
  127.9 41.7 %all-to-all-start.1 = ((bf16[16,32,512]{2,1,0:T(8,128)(2,1)}), bf16[16,32,512]{2,1,0:T(8,128)(2,1)S(1)}, u32[]{:S(2)}, u32[]{:S(2)}) async-start(bf16[16,32,512]{2,1,0:T(8,128)(2,1)} %bitcast.9), calls=%async_computation.1 | async-start | bytes 1048576 | tf_op jit(solution)/shard_map/all_to_all | solution.py:402
  132.4 7.5 %collective-permute-start.4 = (f32[72,128]{1,0:T(8,128)S(1)}, f32[72,128]{1,0:T(8,128)S(1)}, u32[]{:S(2)}, u32[]{:S(2)}) collective-permute-start(f32[72,128]{1,0:T(8,128)S(1)} %pad_bitcast_fusion), channel_id=1, source_target_pairs={{0,2},{2,0},{4,6},{6,4},{8,10},{10,8},{12,14},{14,12},{16,18},{18,... | collective-permute-start | bytes 110600 | tf_op jit(solution)/shard_map/ppermute | solution.py:223
  140.0 4.7 %collective-permute-start.5 = (f32[72,128]{1,0:T(8,128)S(1)}, f32[72,128]{1,0:T(8,128)S(1)}, u32[]{:S(2)}, u32[]{:S(2)}) collective-permute-start(f32[72,128]{1,0:T(8,128)S(1)} %fusion.48), channel_id=1, source_target_pairs={{0,4},{2,6},{4,0},{6,2},{8,12},{10,14},{12,8},{14,10},{16,20},{18,... | collective-permute-start | bytes 110600 | tf_op jit(solution)/shard_map/ppermute | solution.py:223
  144.7 6.9 %collective-permute-start.6 = (f32[72,128]{1,0:T(8,128)S(1)}, f32[72,128]{1,0:T(8,128)S(1)}, u32[]{:S(2)}, u32[]{:S(2)}) collective-permute-start(f32[72,128]{1,0:T(8,128)S(1)} %fusion.109), channel_id=1, source_target_pairs={{0,8},{2,10},{4,12},{6,14},{8,0},{10,2},{12,4},{14,6},{16,24},{18,... | collective-permute-start | bytes 110600 | tf_op jit(solution)/shard_map/ppermute | solution.py:223
  151.6 12.8 %collective-permute-start.7 = (f32[72,128]{1,0:T(8,128)S(1)}, f32[72,128]{1,0:T(8,128)S(1)}, u32[]{:S(2)}, u32[]{:S(2)}) collective-permute-start(f32[72,128]{1,0:T(8,128)S(1)} %add.198), channel_id=1, source_target_pairs={{0,16},{2,18},{4,20},{6,22},{8,24},{10,26},{12,28},{14,30},{16,0},... | collective-permute-start | bytes 110600 | tf_op jit(solution)/shard_map/ppermute | solution.py:223
  398.9 4.7 %copy-start.7 = (bf16[1536,768]{1,0:T(8,128)(2,1)S(1)}, bf16[1536,768]{1,0:T(8,128)(2,1)}, u32[]{:S(2)}) copy-start(bf16[1536,768]{1,0:T(8,128)(2,1)} %get-tuple-element.93) | copy-start | bytes 7077892
  409.6 4.4 %copy-start.1 = (bf16[1536,768]{1,0:T(8,128)(2,1)S(1)}, bf16[1536,768]{1,0:T(8,128)(2,1)}, u32[]{:S(2)}) copy-start(bf16[1536,768]{1,0:T(8,128)(2,1)} %param.47) | copy-start | bytes 7077892
  (38 other events, 77.3 us)
Sparse Core Ops, SparseCore 0:
  123.4 275.4 all-reduce.4
